TPU v7x, 32 devices: a whole 2x2x4 slice. The times are simulated.
32 devices in a mesh: row: 2 (over core), col: 4 (over y, x), depth: 4 (over z).
Axes of the slice: x: 2, y: 2, z: 4, core: 2. Of those that a mesh axis runs over, the one named last changes fastest.
Arguments:
- traces: bfloat16 [32768, 16384], P(('col', 'depth'), 'row'), may hold values from -0.03125 to 0.03125
- features: bfloat16 [32768, 2048], P(('col', 'depth'), 'row'), may hold values from -6 to 6
- next_features: bfloat16 [32768, 2048], P(('col', 'depth'), 'row'), may hold values from -6 to 6
Outputs:
- panels: float32 [16384, 2048], P('row', ('col', 'depth'))
All inputs are finite; a program needn't handle non-finite values.
Results may differ from a plain program's by a relative error of at most 0.0028.
Values may be sent and summed in bfloat16 or wider, within the bound.
No kernel may reach another device: no remote copies, remote signals or barrier semaphores. Data moves between devices by JAX's collectives and lax.ppermute only.
A program may use at most 192 MiB of HBM per device.

v0:
```python
import jax
import jax.numpy as jnp
from jax import lax
from jax.sharding import PartitionSpec as P

DISCOUNT = 0.99


def outer_sum(left, right):
    return lax.dot_general(
        left, right, (((0,), (0,)), ((), ())), preferred_element_type=jnp.float32
    )


def shards(traces, features, next_features):
    differences = (
        features.astype(jnp.float32) - DISCOUNT * next_features.astype(jnp.float32)
    ).astype(jnp.bfloat16)
    partial_sum = outer_sum(traces, lax.all_gather(differences, "row", axis=1, tiled=True))
    col_block = lax.psum_scatter(partial_sum, "col", scatter_dimension=1, tiled=True)
    return lax.psum_scatter(col_block, "depth", scatter_dimension=1, tiled=True)


def solution(mesh):
    return jax.shard_map(
        shards,
        mesh=mesh,
        in_specs=(
            P(("col", "depth"), "row"),
            P(("col", "depth"), "row"),
            P(("col", "depth"), "row"),
        ),
        out_specs=P("row", ("col", "depth")),
        check_vma=False,
    )
```

profile of v0, /device:TPU:0, one launch (start us, length us, event | category | flops | bytes accessed | tf_op | source)
XLA Modules:
  0.0 970.8 jit_solution(9471347879823973983)
XLA Ops:
  6.5 0.0 all-gather.2.cloned.1.call-start
  6.5 7.6 subtract_convert_fusion
  14.2 0.0 all-gather.2.cloned.1.call-update
  14.2 0.0 reduce-scatter.7.cloned.1.call-start
  14.2 22.7 %all-gather.2.cloned.1.call-done = bf16[2048,2048]{1,0:T(8,128)(2,1)} async-done(((bf16[2048,1024]{1,0:T(8,128)(2,1)}), bf16[2048,2048]{1,0:T(8,128)(2,1)}) %all-gather.2.cloned.1.call-update) | async-done | bytes 8388624 | tf_op jit(solution)/shard_map/all_gather | solution.py:19
  36.9 79.5 %convolution_bitcast_fusion = f32[8192,2048]{0,1:T(8,128)} fusion(bf16[2048,2048]{1,0:T(8,128)(2,1)} %all-gather.2.cloned.1.call-done, bf16[2048,8192]{1,0:T(8,128)(2,1)} %param.3), kind=kOutput, calls=%fused_computation | convolution fusion | flops 68719476736 | bytes 109051904 | tf_op jit(solution)/shard_map/dot_general | solution.py:10
  116.4 0.0 reduce-scatter.7.cloned.1.call-update
  116.4 0.0 reduce-scatter.5.cloned.1.call-start
  116.4 559.6 %reduce-scatter.7.cloned.1.call-done = f32[8192,512]{0,1:T(8,128)} async-done(((f32[8192,2048]{0,1:T(8,128)}), f32[8192,512]{0,1:T(8,128)}) %reduce-scatter.7.cloned.1.call-update) | async-done | bytes 16777232
  676.0 0.0 reduce-scatter.5.cloned.1.call-update
  676.0 282.6 %reduce-scatter.5.cloned.1.call-done = f32[8192,128]{0,1:T(8,128)} async-done(((f32[8192,512]{0,1:T(8,128)}), f32[8192,128]{0,1:T(8,128)}) %reduce-scatter.5.cloned.1.call-update) | async-done | bytes 4194320 | tf_op jit(solution)/shard_map/reduce_scatter | solution.py:21
  958.7 5.6 copy.5
Async XLA Ops:
  6.5 30.4 %all-gather.2.cloned.1.call-start = ((), (), s32[]{:S(2)}) async-start(), calls=%async_computation.2 | async-start | bytes 12582912 | tf_op jit(solution)/shard_map/all_gather | solution.py:19
  14.2 661.8 %reduce-scatter.7.cloned.1.call-start = ((), (), s32[]{:S(2)}) async-start(), calls=%async_computation.4 | async-start | bytes 83886080
  116.4 842.3 %reduce-scatter.5.cloned.1.call-start = ((), (), s32[]{:S(2)}) async-start(), calls=%async_computation.3 | async-start | bytes 20971520 | tf_op jit(solution)/shard_map/reduce_scatter | solution.py:21
Sparse Core Ops, SparseCore 0:
  14.3 22.5 all-gather.1
  116.5 559.4 reduce-scatter.6
  678.4 280.2 reduce-scatter.4
where the time goes:
time: 971 us
  waiting for transfers between devices  865 us (89%)
  matrix products  79.5 us (8%)
  between operations  13.1 us (1%)
    unnamed x4, waiting for transfers between devices  560 us
    reduce_scatter x1, waiting for transfers between devices, shards(): return lax.psum_scatter(col_block, 'depth', scatter_dimension=1, tiled=True)  283 us
    dot_general x1, matrix products, outer_sum(): lax.dot_general(left, right, (((0,), (0,)), ((), ())), preferred_element_...  79.5 us
    all_gather x1, waiting for transfers between devices, shards(): lax.all_gather(differences, 'row', axis=1, tiled=True)  22.7 us
  transfers between devices with their start and end apart: 3, of which 3 were waited for; matrix products, arithmetic and copies ran while one was open for 0% of the time, Pallas kernels for 0%

commit v1 on v0

v1 whole, which is shorter than its diff:
```python
import functools

import jax
import jax.numpy as jnp
from jax import lax
from jax.experimental import pallas as pl
from jax.experimental.pallas import tpu as pltpu
from jax.sharding import PartitionSpec as P

DISCOUNT = 0.99
LANES = 128
VMEM_LIMIT = 56 * 1024 * 1024
BRIEF = pl.CostEstimate(flops=0, bytes_accessed=0, transcendentals=0)

UNITS = (
    ("xlyh", 2),
    ("xlyh", 4),
    ("xlyh", 4),
    ("xlyh", 4),
    ("xlyh", 4),
    ("xlyh", 4),
    ("xlyh", 4),
    ("xlyh", 2),
    ("xlyh", 2),
    ("xlyh", 2),
)
ORDER = (
    0, 1, 2, 0, 3, 1, 0, 4, 2, 1, 5, 3, 0, 2, 6, 4, 1, 3, 0, 7, 5, 2, 4, 8,
    1, 9, 6, 5, 3, 7, 2, 4, 8, 6, 9, 3, 5, 7, 6, 7, 4, 8, 8, 9, 9, 5, 6, 7,
    8, 9,
)

MIRROR = {"x": "y", "y": "x", "l": "l", "h": "h"}


def half(x):
    return x.astype(jnp.bfloat16)


def full(x):
    return x.astype(jnp.float32)


def slot_of(order, bits):
    return bits[order[1]] * 4 + bits[order[2]] * 2 + bits[order[3]]


def product_kernel(orders, group, table, traces, own, other, after, *refs):
    keeps, sends, (held, sems) = refs[:2], refs[2:-2], refs[-2:]
    first = pl.program_id(0) == 0
    tall = traces.shape[1] // 2
    places = (3, 1, 2, 0)
    z_low, z_high = table[8] % 2, table[8] // 2

    def load(source, place):
        start = pl.multiple_of(table[2 * place + 1], group)
        return pltpu.make_async_copy(
            source.at[:, pl.ds(start, group)], held.at[place], sems.at[place]
        )

    @pl.when(first)
    def _():
        for place in places:

            @pl.when(table[2 * place] == 0)
            def _():
                load(own, place).start()

            @pl.when(table[2 * place] != 0)
            def _():
                load(other, place).start()

    def products(place):
        rows = traces[...]
        total = lax.dot_general(
            rows,
            held[place],
            (((0,), (0,)), ((), ())),
            preferred_element_type=jnp.float32,
        )
        pieces = [
            total[:, block * LANES : (block + 1) * LANES]
            for block in range(group // LANES)
        ]
        for chunk, order in enumerate(orders):
            mine = [p[chunk * tall : (chunk + 1) * tall] for p in pieces]
            if order[0] == "l":
                for high in range(len(mine) // 2):
                    bits = {
                        "x": place % 2,
                        "y": place // 2,
                        "h": lax.bitwise_xor(z_high, high),
                    }
                    slot = slot_of(order, bits)
                    even, odd = mine[2 * high], mine[2 * high + 1]
                    keeps[chunk][slot] = jnp.where(z_low == 0, even, odd)
                    sends[0][8 * chunk + slot] = half(jnp.where(z_low == 0, odd, even))
            else:
                for block, piece in enumerate(mine):
                    bits = {
                        "x": place % 2,
                        "y": place // 2,
                        "l": lax.bitwise_xor(z_low, block % 2),
                        "h": lax.bitwise_xor(z_high, block // 2),
                    }
                    slot = slot_of(order, bits)
                    if bits[order[0]]:
                        sends[chunk][slot] = half(piece)
                    else:
                        keeps[chunk][slot] = piece

    @pl.when(first)
    def _():
        for place in places:
            load(own, place).wait()
            products(place)

    @pl.when(jnp.logical_not(first))
    def _():
        for place in places:
            products(place)


def tall_of(first_row, height):
    return 256 if height % 256 == 0 and first_row % 512 == 0 else 128


def unit_products(orders, table, traces, own, other, first_row, height, after):
    tokens = traces.shape[0]
    tall = tall_of(first_row, height)
    group = own.shape[1] // 2
    first = first_row // (2 * tall)

    def block(slots):
        return pl.BlockSpec((slots, tall, LANES), lambda i, table: (0, i, 0))

    def shape(slots, dtype):
        return jax.ShapeDtypeStruct((slots, height, LANES), dtype)

    counts = [16] if orders[0][0] == "l" else [8, 8]
    outs = pl.pallas_call(
        functools.partial(product_kernel, orders, group),
        name="products",
        grid_spec=pltpu.PrefetchScalarGridSpec(
            num_scalar_prefetch=1,
            grid=(height // tall,),
            in_specs=[
                pl.BlockSpec((tokens, 2 * tall), lambda i, table: (0, first + i)),
                pl.BlockSpec(memory_space=pl.ANY),
                pl.BlockSpec(memory_space=pl.ANY),
                pl.BlockSpec(memory_space=pl.ANY),
            ],
            out_specs=[block(8), block(8)] + [block(count) for count in counts],
            scratch_shapes=[
                pltpu.VMEM((4, tokens, group), own.dtype),
                pltpu.SemaphoreType.DMA((4,)),
            ],
        ),
        out_shape=[shape(8, jnp.float32)] * 2
        + [shape(count, jnp.bfloat16) for count in counts],
        cost_estimate=BRIEF,
        compiler_params=pltpu.CompilerParams(vmem_limit_bytes=VMEM_LIMIT),
    )(table, traces, own, other, after)
    return outs[:2], outs[2:]


def sums_kernel(counts, *refs):
    terms, outs = refs[: sum(counts)], refs[sum(counts) + 1 :]
    totals = []
    for chunk in range(2):
        mine = terms[chunk * counts[0] : chunk * counts[0] + counts[chunk]]
        total = mine[0][...]
        for term in mine[1:]:
            total = total + full(term[...])
        totals.append(half(total))
    if len(outs) == 2:
        for out, total in zip(outs, totals):
            out[...] = total
    else:
        slots = totals[0].shape[0]
        outs[0][:slots] = totals[0]
        outs[0][slots:] = totals[1]


def unit_sums(slots, chunks, split, tall, after):
    height = chunks[0][0][0].shape[1]
    terms = chunks[0] + chunks[1]
    specs = [
        pl.BlockSpec((slots, tall, LANES), lambda i, place=start // slots + 1: (place, i, 0))
        for _, start in terms
    ]
    held = slots if split else 2 * slots
    shape = jax.ShapeDtypeStruct((held, height, LANES), jnp.bfloat16)
    block = pl.BlockSpec((held, tall, LANES), lambda i: (0, i, 0))
    return pl.pallas_call(
        functools.partial(sums_kernel, [len(c) for c in chunks]),
        name="sums",
        grid=(height // tall,),
        in_specs=specs + [pl.BlockSpec(memory_space=pl.ANY)],
        out_specs=[block] * (1 + split),
        out_shape=[shape] * (1 + split),
        cost_estimate=BRIEF,
        compiler_params=pltpu.CompilerParams(vmem_limit_bytes=VMEM_LIMIT),
    )(*[array for array, _ in terms], after)


def last_kernel(count, *refs):
    out, done = refs[-2:]
    tall = out.shape[0] // 2
    done[...] = jnp.zeros_like(done)
    for chunk in range(2):
        mine = refs[chunk * count : (chunk + 1) * count]
        total = mine[0][0]
        for term in mine[1:]:
            total = total + full(term[0])
        out[chunk * tall : (chunk + 1) * tall] = total


def unit_last(out, rows, chunks, first_row, tall, after):
    height = chunks[0][0][0].shape[1]
    first = first_row // (2 * tall)
    terms = chunks[0] + chunks[1]
    specs = [
        pl.BlockSpec((1, tall, LANES), lambda i, place=place: (place, i, 0))
        for _, place in terms
    ]
    operands = [array for array, _ in terms] + [after]
    aliases = {}
    if out is not None:
        aliases = {len(operands): 0}
        operands.append(out)
    return pl.pallas_call(
        functools.partial(last_kernel, len(chunks[0])),
        name="last",
        grid=(height // tall,),
        in_specs=specs + [pl.BlockSpec(memory_space=pl.ANY)] * (1 + len(aliases)),
        out_specs=[
            pl.BlockSpec((2 * tall, LANES), lambda i: (first + i, 0)),
            pl.BlockSpec((8, LANES), lambda i: (0, 0)),
        ],
        out_shape=[
            jax.ShapeDtypeStruct((rows, LANES), jnp.float32),
            jax.ShapeDtypeStruct((8, LANES), jnp.float32),
        ],
        input_output_aliases=aliases,
        cost_estimate=BRIEF,
        compiler_params=pltpu.CompilerParams(vmem_limit_bytes=VMEM_LIMIT),
    )(*operands)


def plan(rows):
    steps = rows // (2 * LANES)
    units, order = UNITS, ORDER
    if sum(share for _, share in units) != steps:
        units = (("xlyh", 1),) * steps
        order = [
            unit
            for turn in range(steps + 4)
            for unit in range(turn, turn - 5, -1)
            if 0 <= unit < steps
        ]
    starts, start = {}, 0
    for unit in sorted(range(len(units)), key=lambda u: units[u][1] % 2):
        starts[unit] = start
        start += units[unit][1] * 2 * LANES
    return [
        ((a, "".join(MIRROR[d] for d in a)), starts[unit], share * LANES)
        for unit, (a, share) in enumerate(units)
    ], order


def shards(sizes, traces, features, next_features):
    rows_n, cols_n, depth = sizes
    differences = half(full(features) - DISCOUNT * full(next_features))
    row, col, z = (lax.axis_index(name) for name in ("row", "col", "depth"))
    if rows_n == 2:
        own, flip = differences, row
        other = lax.ppermute(differences, "row", [(0, 1), (1, 0)])
    else:
        whole = lax.all_gather(differences, "row", axis=1, tiled=True)
        own, other = jnp.split(whole, 2, axis=1)
        flip = 0
    group = own.shape[1] // 2
    rows = traces.shape[1]

    entries = []
    for bits in range(4):
        near = lax.bitwise_xor(col, bits)
        entries += [lax.bitwise_xor(near // 2, flip), (near % 2) * group]
    table = jnp.stack(entries + [z]).astype(jnp.int32)

    def swap(v, dim):
        axis, size, bit = {
            "x": ("col", cols_n, 1),
            "y": ("col", cols_n, 2),
            "l": ("depth", depth, 1),
            "h": ("depth", depth, 2),
        }[dim]
        return lax.ppermute(v, axis, [(i, i ^ bit) for i in range(size)])

    units, order = plan(rows)
    terms = [None] * len(units)
    stages = [0] * len(units)
    after, out = table, None
    for unit in order:
        orders, first_row, height = units[unit]
        stage, tall = stages[unit], tall_of(first_row, height)
        stages[unit] += 1
        if stage == 4:
            out, after = unit_last(out, rows, terms[unit], first_row, tall, after)
            continue
        dims = [o[stage] for o in orders]
        slots = 8 >> stage
        if stage == 0:
            keeps, sends = unit_products(
                orders, table, traces, own, other, first_row, height, after
            )
            terms[unit] = [[(keep, 0)] for keep in keeps]
        else:
            sends = unit_sums(slots, terms[unit], dims[0] != dims[1], tall, after)
        after = sends[0]
        got = [swap(send, dim) for send, dim in zip(sends, dims)]
        for chunk in range(2):
            arrived = (got[chunk], 0) if len(got) == 2 else (got[0], slots * chunk)
            terms[unit][chunk].append(arrived)
    return out


def solution(mesh):
    sizes = tuple(mesh.shape[name] for name in ("row", "col", "depth"))
    spec = P(("col", "depth"), "row")
    return jax.shard_map(
        functools.partial(shards, sizes),
        mesh=mesh,
        in_specs=(spec, spec, spec),
        out_specs=P("row", ("col", "depth")),
        check_vma=False,
    )
```

time: 971 us -> 387 us (0.40)
  waiting for transfers between devices: 865 us -> 58.2 us
  Pallas kernels: 0 us -> 226 us
  matrix products: 79.5 us -> 0 us
  starting transfers between devices: 0.09 us -> 74.4 us
  between operations: 13.1 us -> 1.16 us
    unnamed x4 -> x0, waiting for transfers between devices: 560 us -> none
    reduce_scatter x1 -> x0, waiting for transfers between devices: 283 us -> none  [shards(): return lax.psum_scatter(col_block, 'depth', scatter_dimension=1, tiled=True)]
    pallas_call x0 -> x50, Pallas kernels: none -> 226 us  [the longest x10 137 us: unit_products(): pl.pallas_call(functools.partial(product_kernel, orders, group), name='pr...]
    dot_general x1 -> x0, matrix products: 79.5 us -> none  [outer_sum(): lax.dot_general(left, right, (((0,), (0,)), ((), ())), preferred_element_...]
    ppermute x0 -> x61, starting transfers between devices: none -> 74.4 us  [the longest x60 73.9 us: swap(): return lax.ppermute(v, axis, [(i, i ^ bit) for i in range(size)])]
    ppermute x0 -> x61, waiting for transfers between devices: none -> 58.2 us  [the longest x60 51.6 us: swap(): return lax.ppermute(v, axis, [(i, i ^ bit) for i in range(size)])]
    all_gather x1 -> x0, waiting for transfers between devices: 22.7 us -> none  [shards(): lax.all_gather(differences, 'row', axis=1, tiled=True)]
    unnamed x0 -> x158, local copies, waits for them, and re-layouts: none -> 13.3 us
  transfers between devices with their start and end apart: 3 -> 61, of which waited for: 3 -> 16; matrix products, arithmetic and copies ran while one was open for 0% -> 0% of each run, Pallas kernels for 0% -> 52%
where the time goes in v1:
time: 387 us; the launch traced here: 381 us
  Pallas kernels  226 us (58%)
  starting transfers between devices  74.4 us (19%)
  waiting for transfers between devices  58.2 us (15%)
  local copies, waits for them, and re-layouts  13.9 us (4%)
  other arithmetic  7.62 us (2%)
    pallas_call x10, Pallas kernels, unit_products(): pl.pallas_call(functools.partial(product_kernel, orders, group), name='pr...  137 us
    ppermute x60, starting transfers between devices, swap(): return lax.ppermute(v, axis, [(i, i ^ bit) for i in range(size)])  73.9 us
    pallas_call x30, Pallas kernels, unit_sums(): pl.pallas_call(functools.partial(sums_kernel, [len(c) for c in chunks]),...  67.8 us
    ppermute x60, waiting for transfers between devices, swap(): return lax.ppermute(v, axis, [(i, i ^ bit) for i in range(size)])  51.6 us
    pallas_call x10, Pallas kernels, unit_last(): pl.pallas_call(functools.partial(last_kernel, len(chunks[0])), name='last...  20.9 us
    unnamed x158, local copies, waits for them, and re-layouts  13.3 us
  transfers between devices with their start and end apart: 61, of which 16 were waited for; matrix products, arithmetic and copies ran while one was open for 0% of the time, Pallas kernels for 52%

profile of v1, /device:TPU:0, one launch (start us, length us, event | category | flops | bytes accessed | tf_op | source)
XLA Modules:
  0.0 381.1 jit_solution(11946008979464433056)
XLA Ops:
  0.0 7.6 %subtract_convert_fusion.own = bf16[2048,1024]{1,0:T(8,128)(2,1)} fusion(bf16[2048,1024]{1,0:T(8,128)(2,1)} %param.5, bf16[2048,1024]{1,0:T(8,128)(2,1)} %param.4), kind=kLoop, calls=%fused_computation | loop fusion | flops 10485760 | bytes 12582912 | tf_op jit(solution)/shard_map/convert_element_type | solution.py:37
  8.7 6.5 %collective-permute-done.other = bf16[2048,1024]{1,0:T(8,128)(2,1)} collective-permute-done((bf16[2048,1024]{1,0:T(8,128)(2,1)}, bf16[2048,1024]{1,0:T(8,128)(2,1)}, u32[]{:S(2)}, u32[]{:S(2)}) %collective-permute-start) | collective-permute-done | bytes 4194336 | tf_op jit(solution)/shard_map/ppermute | solution.py:278
  15.2 10.5 %products.10 = (f32[8,256,128]{2,1,0:T(8,128)}, f32[8,256,128]{2,1,0:T(8,128)}, bf16[8,256,128]{2,1,0:T(8,128)(2,1)}, bf16[8,256,128]{2,1,0:T(8,128)(2,1)}) custom-call(s32[9]{0:T(128)} %stack.39.table.after, bf16[2048,8192]{1,0:T(8,128)(2,1)} %traces.19, bf16[2048,1024]{1,0:T(8,128)(2,1)} %subtract_convert_fusion.own, ...), custom_call_target="tpu_custom_call" | custom-call | tf_op jit(solution)/shard_map/products/pallas_call | solution.py:141
  25.7 15.9 %products.11 = (f32[8,512,128]{2,1,0:T(8,128)}, f32[8,512,128]{2,1,0:T(8,128)}, bf16[8,512,128]{2,1,0:T(8,128)(2,1)}, bf16[8,512,128]{2,1,0:T(8,128)(2,1)}) custom-call(s32[9]{0:T(128)} %stack.39.table.after, bf16[2048,8192]{1,0:T(8,128)(2,1)} %traces.19, bf16[2048,1024]{1,0:T(8,128)(2,1)} %subtract_convert_fusion.own, ...), custom_call_target="tpu_custom_call" | custom-call | tf_op jit(solution)/shard_map/products/pallas_call | solution.py:141
  41.6 3.0 collective-permute-start.2
  46.7 15.9 %products.12 = (f32[8,512,128]{2,1,0:T(8,128)}, f32[8,512,128]{2,1,0:T(8,128)}, bf16[8,512,128]{2,1,0:T(8,128)(2,1)}, bf16[8,512,128]{2,1,0:T(8,128)(2,1)}) custom-call(s32[9]{0:T(128)} %stack.39.table.after, bf16[2048,8192]{1,0:T(8,128)(2,1)} %traces.19, bf16[2048,1024]{1,0:T(8,128)(2,1)} %subtract_convert_fusion.own, ...), custom_call_target="tpu_custom_call" | custom-call | tf_op jit(solution)/shard_map/products/pallas_call | solution.py:141
  62.6 2.0 collective-permute-start.7
  64.6 15.4 %collective-permute-done.4.refs_3_.refs_4_.refs_5_.refs_6_ = bf16[8,256,128]{2,1,0:T(8,128)(2,1)S(1)} collective-permute-done((bf16[8,256,128]{2,1,0:T(8,128)(2,1)S(1)}, bf16[8,256,128]{2,1,0:T(8,128)(2,1)S(1)}, u32[]{:S(2)}, u32[]{:S(2)}) %collective-permute-start.4) | collective-permute-done | bytes 524320 | tf_op jit(solution)/shard_map/ppermute | solution.py:299
  80.0 2.0 collective-permute-start.6
  82.8 2.2 sums.30.after
  86.6 15.9 %products.13 = (f32[8,512,128]{2,1,0:T(8,128)}, f32[8,512,128]{2,1,0:T(8,128)}, bf16[8,512,128]{2,1,0:T(8,128)(2,1)}, bf16[8,512,128]{2,1,0:T(8,128)(2,1)}) custom-call(s32[9]{0:T(128)} %stack.39.table.after, bf16[2048,8192]{1,0:T(8,128)(2,1)} %traces.19, bf16[2048,1024]{1,0:T(8,128)(2,1)} %subtract_convert_fusion.own, ...), custom_call_target="tpu_custom_call" | custom-call | tf_op jit(solution)/shard_map/products/pallas_call | solution.py:141
  103.8 2.7 sums.31.refs_6_
  109.3 2.0 sums.32
  111.2 16.1 %products.14 = (f32[8,512,128]{2,1,0:T(8,128)}, f32[8,512,128]{2,1,0:T(8,128)}, bf16[8,512,128]{2,1,0:T(8,128)(2,1)}, bf16[8,512,128]{2,1,0:T(8,128)(2,1)}) custom-call(s32[9]{0:T(128)} %stack.39.table.after, bf16[2048,8192]{1,0:T(8,128)(2,1)} %traces.19, bf16[2048,1024]{1,0:T(8,128)(2,1)} %subtract_convert_fusion.own, ...), custom_call_target="tpu_custom_call" | custom-call | tf_op jit(solution)/shard_map/products/pallas_call | solution.py:141
  128.3 2.7 sums.33.refs_6_
  134.4 2.4 sums.34
  136.7 15.7 %products.15 = (f32[8,512,128]{2,1,0:T(8,128)}, f32[8,512,128]{2,1,0:T(8,128)}, bf16[8,512,128]{2,1,0:T(8,128)(2,1)}, bf16[8,512,128]{2,1,0:T(8,128)(2,1)}) custom-call(s32[9]{0:T(128)} %stack.39.table.after, bf16[2048,8192]{1,0:T(8,128)(2,1)} %traces.19, bf16[2048,1024]{1,0:T(8,128)(2,1)} %subtract_convert_fusion.own, ...), custom_call_target="tpu_custom_call" | custom-call | tf_op jit(solution)/shard_map/products/pallas_call | solution.py:141
  153.8 2.8 sums.35.refs_8_
  158.1 4.0 %collective-permute-done.15.refs_7_.refs_8_ = bf16[2,256,128]{2,1,0:T(8,128)(2,1)S(1)} collective-permute-done((bf16[2,256,128]{2,1,0:T(8,128)(2,1)S(1)}, bf16[2,256,128]{2,1,0:T(8,128)(2,1)S(1)}, u32[]{:S(2)}, u32[]{:S(2)}) %collective-permute-start.15) | collective-permute-done | bytes 131104 | tf_op jit(solution)/shard_map/ppermute | solution.py:299
  163.6 4.9 %collective-permute-done.14.refs_3_ = bf16[2,256,128]{2,1,0:T(8,128)(2,1)S(1)} collective-permute-done((bf16[2,256,128]{2,1,0:T(8,128)(2,1)S(1)}, bf16[2,256,128]{2,1,0:T(8,128)(2,1)S(1)}, u32[]{:S(2)}, u32[]{:S(2)}) %collective-permute-start.14) | collective-permute-done | bytes 131104 | tf_op jit(solution)/shard_map/ppermute | solution.py:299
  171.9 2.7 collective-permute-start.24
  176.6 2.9 collective-permute-done.24.refs_4_.refs_9_
  180.9 2.4 sums.37
  184.8 15.7 %products.16 = (f32[8,512,128]{2,1,0:T(8,128)}, f32[8,512,128]{2,1,0:T(8,128)}, bf16[8,512,128]{2,1,0:T(8,128)(2,1)}, bf16[8,512,128]{2,1,0:T(8,128)(2,1)}) custom-call(s32[9]{0:T(128)} %stack.39.table.after, bf16[2048,8192]{1,0:T(8,128)(2,1)} %traces.19, bf16[2048,1024]{1,0:T(8,128)(2,1)} %subtract_convert_fusion.own, ...), custom_call_target="tpu_custom_call" | custom-call | tf_op jit(solution)/shard_map/products/pallas_call | solution.py:141
  200.6 2.8 sums.38.refs_8_
  203.4 4.1 %collective-permute-start.19 = (bf16[8,512,128]{2,1,0:T(8,128)(2,1)}, bf16[8,512,128]{2,1,0:T(8,128)(2,1)S(1)}, u32[]{:S(2)}, u32[]{:S(2)}) collective-permute-start(bf16[8,512,128]{2,1,0:T(8,128)(2,1)} %sums.38.refs_8_), channel_id=1, source_target_pairs={{0,1},{1,0},{2,3},{3,2},{4,5},{5,4},{6,7},{7,6},{8,9},{9,8},{10,11... | collective-permute-start | bytes 3145736 | tf_op jit(solution)/shard_map/ppermute | solution.py:299
  210.7 2.1 sums.39.refs_6_
  212.8 2.6 sums.40
  215.5 1.9 last.10
  217.4 10.5 %products.17 = (f32[8,256,128]{2,1,0:T(8,128)}, f32[8,256,128]{2,1,0:T(8,128)}, bf16[8,256,128]{2,1,0:T(8,128)(2,1)}, bf16[8,256,128]{2,1,0:T(8,128)(2,1)}) custom-call(s32[9]{0:T(128)} %stack.39.table.after, bf16[2048,8192]{1,0:T(8,128)(2,1)} %traces.19, bf16[2048,1024]{1,0:T(8,128)(2,1)} %subtract_convert_fusion.own, ...), custom_call_target="tpu_custom_call" | custom-call | tf_op jit(solution)/shard_map/products/pallas_call | solution.py:141
  228.0 2.8 sums.41.refs_8_
  230.8 4.5 %collective-permute-done.20.refs_3_ = bf16[2,512,128]{2,1,0:T(8,128)(2,1)S(1)} collective-permute-done((bf16[2,512,128]{2,1,0:T(8,128)(2,1)S(1)}, bf16[2,512,128]{2,1,0:T(8,128)(2,1)S(1)}, u32[]{:S(2)}, u32[]{:S(2)}) %collective-permute-start.20) | collective-permute-done | bytes 262176 | tf_op jit(solution)/shard_map/ppermute | solution.py:299
  236.9 2.1 sums.42.refs_6_
  239.1 2.0 collective-permute-start.35
  241.1 2.6 sums.43
  247.4 10.5 %products.18 = (f32[8,256,128]{2,1,0:T(8,128)}, f32[8,256,128]{2,1,0:T(8,128)}, bf16[8,256,128]{2,1,0:T(8,128)(2,1)}, bf16[8,256,128]{2,1,0:T(8,128)(2,1)}) custom-call(s32[9]{0:T(128)} %stack.39.table.after, bf16[2048,8192]{1,0:T(8,128)(2,1)} %traces.19, bf16[2048,1024]{1,0:T(8,128)(2,1)} %subtract_convert_fusion.own, ...), custom_call_target="tpu_custom_call" | custom-call | tf_op jit(solution)/shard_map/products/pallas_call | solution.py:141
  257.9 2.2 last.11
  260.1 10.6 %products.19 = (f32[8,256,128]{2,1,0:T(8,128)}, f32[8,256,128]{2,1,0:T(8,128)}, bf16[8,256,128]{2,1,0:T(8,128)(2,1)}, bf16[8,256,128]{2,1,0:T(8,128)(2,1)}) custom-call(s32[9]{0:T(128)} %stack.39.table.after, bf16[2048,8192]{1,0:T(8,128)(2,1)} %traces.19, bf16[2048,1024]{1,0:T(8,128)(2,1)} %subtract_convert_fusion.own, ...), custom_call_target="tpu_custom_call" | custom-call | tf_op jit(solution)/shard_map/products/pallas_call | solution.py:141
  271.4 2.7 sums.44.refs_6_
  274.2 2.1 collective-permute-start.30
  276.2 3.8 collective-permute-done.33.refs_3_
  284.2 2.4 sums.45
  286.6 2.2 sums.46.refs_4_
  288.8 2.3 sums.47.refs_10_
  293.1 2.5 collective-permute-start.47
  295.5 3.3 collective-permute-done.32.refs_3_.refs_4_.refs_5_.refs_6_
  301.2 2.2 last.12
  303.5 2.1 sums.48.refs_4_
  305.5 2.2 sums.49.refs_6_
  308.7 2.3 sums.50
  311.1 5.9 %collective-permute-done.47.refs_4_.refs_9_ = bf16[2,512,128]{2,1,0:T(8,128)(2,1)S(1)} collective-permute-done((bf16[2,512,128]{2,1,0:T(8,128)(2,1)}, bf16[2,512,128]{2,1,0:T(8,128)(2,1)S(1)}, u32[]{:S(2)}, u32[]{:S(2)}) %collective-permute-start.47) | collective-permute-done | bytes 262176 | tf_op jit(solution)/shard_map/ppermute | solution.py:299
  318.8 2.2 sums.51.refs_10_
  321.0 2.0 collective-permute-start.41
  324.4 2.2 last.13
  326.6 2.1 sums.52.refs_6_
  328.7 2.0 sums.53
  332.9 2.1 sums.54.refs_8_
  339.7 2.2 last.14
  342.7 2.0 sums.56
  354.6 2.0 sums.58
  367.8 2.2 last.15
  370.7 2.2 last.16
  373.6 1.9 last.17
  376.2 1.9 last.18
  (268 shorter events, 82.0 us)
Async XLA Ops:
  7.6 7.6 %collective-permute-start = (bf16[2048,1024]{1,0:T(8,128)(2,1)}, bf16[2048,1024]{1,0:T(8,128)(2,1)}, u32[]{:S(2)}, u32[]{:S(2)}) collective-permute-start(bf16[2048,1024]{1,0:T(8,128)(2,1)} %subtract_convert_fusion.own), channel_id=1, source_target_pairs={{0,16},{16,0},{1,17},{17,1},{2,18},{18,2},{3,19},{19,3},{4,20},{20... | collective-permute-start | bytes 12582920 | tf_op jit(solution)/shard_map/ppermute | solution.py:278
  41.6 60.8 %collective-permute-start.2 = (bf16[8,512,128]{2,1,0:T(8,128)(2,1)}, bf16[8,512,128]{2,1,0:T(8,128)(2,1)S(1)}, u32[]{:S(2)}, u32[]{:S(2)}) collective-permute-start(bf16[8,512,128]{2,1,0:T(8,128)(2,1)} %get-tuple-element.88), channel_id=1, source_target_pairs={{0,8},{4,12},{8,0},{12,4},{1,9},{5,13},{9,1},{13,5},{2,10},{6,14},... | collective-permute-start | bytes 3145736 | tf_op jit(solution)/shard_map/ppermute | solution.py:299
  44.6 57.9 %collective-permute-start.1 = (bf16[8,512,128]{2,1,0:T(8,128)(2,1)}, bf16[8,512,128]{2,1,0:T(8,128)(2,1)S(1)}, u32[]{:S(2)}, u32[]{:S(2)}) collective-permute-start(bf16[8,512,128]{2,1,0:T(8,128)(2,1)} %get-tuple-element.86.after), channel_id=1, source_target_pairs={{0,4},{4,0},{8,12},{12,8},{1,5},{5,1},{9,13},{13,9},{2,6},{6,2},{1... | collective-permute-start | bytes 3145736 | tf_op jit(solution)/shard_map/ppermute | solution.py:299
  46.1 33.9 %collective-permute-start.4 = (bf16[8,256,128]{2,1,0:T(8,128)(2,1)S(1)}, bf16[8,256,128]{2,1,0:T(8,128)(2,1)S(1)}, u32[]{:S(2)}, u32[]{:S(2)}) collective-permute-start(bf16[8,256,128]{2,1,0:T(8,128)(2,1)S(1)} %copy-done.74), channel_id=1, source_target_pairs={{0,8},{4,12},{8,0},{12,4},{1,9},{5,13},{9,1},{13,5},{2,10},{6,14},... | collective-permute-start | bytes 1572872 | tf_op jit(solution)/shard_map/ppermute | solution.py:299
  46.6 35.4 %collective-permute-start.3 = (bf16[8,256,128]{2,1,0:T(8,128)(2,1)S(1)}, bf16[8,256,128]{2,1,0:T(8,128)(2,1)S(1)}, u32[]{:S(2)}, u32[]{:S(2)}) collective-permute-start(bf16[8,256,128]{2,1,0:T(8,128)(2,1)S(1)} %copy-done.50), channel_id=1, source_target_pairs={{0,4},{4,0},{8,12},{12,8},{1,5},{5,1},{9,13},{13,9},{2,6},{6,2},{1... | collective-permute-start | bytes 1572872 | tf_op jit(solution)/shard_map/ppermute | solution.py:299
  62.6 64.8 %collective-permute-start.7 = (bf16[8,512,128]{2,1,0:T(8,128)(2,1)}, bf16[8,512,128]{2,1,0:T(8,128)(2,1)S(1)}, u32[]{:S(2)}, u32[]{:S(2)}) collective-permute-start(bf16[8,512,128]{2,1,0:T(8,128)(2,1)} %get-tuple-element.96), channel_id=1, source_target_pairs={{0,8},{4,12},{8,0},{12,4},{1,9},{5,13},{9,1},{13,5},{2,10},{6,14},... | collective-permute-start | bytes 3145736 | tf_op jit(solution)/shard_map/ppermute | solution.py:299
  80.0 47.4 %collective-permute-start.6 = (bf16[8,512,128]{2,1,0:T(8,128)(2,1)}, bf16[8,512,128]{2,1,0:T(8,128)(2,1)}, u32[]{:S(2)}, u32[]{:S(2)}) collective-permute-start(bf16[8,512,128]{2,1,0:T(8,128)(2,1)} %get-tuple-element.92.refs_4_), channel_id=1, source_target_pairs={{0,4},{4,0},{8,12},{12,8},{1,5},{5,1},{9,13},{13,9},{2,6},{6,2},{1... | collective-permute-start | bytes 3145736 | tf_op jit(solution)/shard_map/ppermute | solution.py:299
  85.0 23.4 %collective-permute-start.8 = (bf16[8,256,128]{2,1,0:T(8,128)(2,1)}, bf16[8,256,128]{2,1,0:T(8,128)(2,1)S(1)}, u32[]{:S(2)}, u32[]{:S(2)}) collective-permute-start(bf16[8,256,128]{2,1,0:T(8,128)(2,1)} %sums.30.after), channel_id=1, source_target_pairs={{0,1},{1,0},{2,3},{3,2},{4,5},{5,4},{6,7},{7,6},{8,9},{9,8},{10,11... | collective-permute-start | bytes 1572872 | tf_op jit(solution)/shard_map/ppermute | solution.py:299
  106.5 26.7 %collective-permute-start.5 = (bf16[8,512,128]{2,1,0:T(8,128)(2,1)}, bf16[8,512,128]{2,1,0:T(8,128)(2,1)S(1)}, u32[]{:S(2)}, u32[]{:S(2)}) collective-permute-start(bf16[8,512,128]{2,1,0:T(8,128)(2,1)} %sums.31.refs_6_), channel_id=1, source_target_pairs={{0,1},{1,0},{2,3},{3,2},{4,5},{5,4},{6,7},{7,6},{8,9},{9,8},{10,11... | collective-permute-start | bytes 3145736 | tf_op jit(solution)/shard_map/ppermute | solution.py:299
  106.9 45.6 %collective-permute-start.17 = (bf16[8,512,128]{2,1,0:T(8,128)(2,1)}, bf16[8,512,128]{2,1,0:T(8,128)(2,1)S(1)}, u32[]{:S(2)}, u32[]{:S(2)}) collective-permute-start(bf16[8,512,128]{2,1,0:T(8,128)(2,1)} %get-tuple-element.107), channel_id=1, source_target_pairs={{0,8},{4,12},{8,0},{12,4},{1,9},{5,13},{9,1},{13,5},{2,10},{6,14},... | collective-permute-start | bytes 3145736 | tf_op jit(solution)/shard_map/ppermute | solution.py:299
  108.5 44.1 %collective-permute-start.16 = (bf16[8,512,128]{2,1,0:T(8,128)(2,1)}, bf16[8,512,128]{2,1,0:T(8,128)(2,1)S(1)}, u32[]{:S(2)}, u32[]{:S(2)}) collective-permute-start(bf16[8,512,128]{2,1,0:T(8,128)(2,1)} %get-tuple-element.93.refs_4_), channel_id=1, source_target_pairs={{0,4},{4,0},{8,12},{12,8},{1,5},{5,1},{9,13},{13,9},{2,6},{6,2},{1... | collective-permute-start | bytes 3145736 | tf_op jit(solution)/shard_map/ppermute | solution.py:299
  131.0 40.8 %collective-permute-start.13 = (bf16[8,512,128]{2,1,0:T(8,128)(2,1)}, bf16[8,512,128]{2,1,0:T(8,128)(2,1)S(1)}, u32[]{:S(2)}, u32[]{:S(2)}) collective-permute-start(bf16[8,512,128]{2,1,0:T(8,128)(2,1)} %sums.33.refs_6_), channel_id=1, source_target_pairs={{0,1},{1,0},{2,3},{3,2},{4,5},{5,4},{6,7},{7,6},{8,9},{9,8},{10,11... | collective-permute-start | bytes 3145736 | tf_op jit(solution)/shard_map/ppermute | solution.py:299
  132.6 41.9 %collective-permute-start.12 = (bf16[8,512,128]{2,1,0:T(8,128)(2,1)}, bf16[8,512,128]{2,1,0:T(8,128)(2,1)S(1)}, u32[]{:S(2)}, u32[]{:S(2)}) collective-permute-start(bf16[8,512,128]{2,1,0:T(8,128)(2,1)} %get-tuple-element.103), channel_id=1, source_target_pairs={{0,8},{4,12},{8,0},{12,4},{1,9},{5,13},{9,1},{13,5},{2,10},{6,14},... | collective-permute-start | bytes 3145736 | tf_op jit(solution)/shard_map/ppermute | solution.py:299
  133.1 42.4 %collective-permute-start.11 = (bf16[8,512,128]{2,1,0:T(8,128)(2,1)}, bf16[8,512,128]{2,1,0:T(8,128)(2,1)S(1)}, u32[]{:S(2)}, u32[]{:S(2)}) collective-permute-start(bf16[8,512,128]{2,1,0:T(8,128)(2,1)} %get-tuple-element.98.refs_4_), channel_id=1, source_target_pairs={{0,4},{4,0},{8,12},{12,8},{1,5},{5,1},{9,13},{13,9},{2,6},{6,2},{1... | collective-permute-start | bytes 3145736 | tf_op jit(solution)/shard_map/ppermute | solution.py:299
  156.6 22.9 %copy-start.68 = (bf16[2,512,128]{2,1,0:T(8,128)(2,1)S(1)}, bf16[2,512,128]{2,1,0:T(8,128)(2,1)}, u32[]{:S(2)}) copy-start(bf16[2,512,128]{2,1,0:T(8,128)(2,1)} %get-tuple-element.99.after) | copy-start | bytes 786436
  156.6 51.6 %collective-permute-start.25 = (bf16[8,512,128]{2,1,0:T(8,128)(2,1)}, bf16[8,512,128]{2,1,0:T(8,128)(2,1)S(1)}, u32[]{:S(2)}, u32[]{:S(2)}) collective-permute-start(bf16[8,512,128]{2,1,0:T(8,128)(2,1)} %sums.35.refs_8_), channel_id=1, source_target_pairs={{0,1},{1,0},{2,3},{3,2},{4,5},{5,4},{6,7},{7,6},{8,9},{9,8},{10,11... | collective-permute-start | bytes 3145736 | tf_op jit(solution)/shard_map/ppermute | solution.py:299
  157.1 5.0 %collective-permute-start.15 = (bf16[2,256,128]{2,1,0:T(8,128)(2,1)S(1)}, bf16[2,256,128]{2,1,0:T(8,128)(2,1)S(1)}, u32[]{:S(2)}, u32[]{:S(2)}) collective-permute-start(bf16[2,256,128]{2,1,0:T(8,128)(2,1)S(1)} %copy-done.78), channel_id=1, source_target_pairs={{0,4},{4,0},{8,12},{12,8},{1,5},{5,1},{9,13},{13,9},{2,6},{6,2},{1... | collective-permute-start | bytes 393224 | tf_op jit(solution)/shard_map/ppermute | solution.py:299
  162.1 6.4 %collective-permute-start.14 = (bf16[2,256,128]{2,1,0:T(8,128)(2,1)S(1)}, bf16[2,256,128]{2,1,0:T(8,128)(2,1)S(1)}, u32[]{:S(2)}, u32[]{:S(2)}) collective-permute-start(bf16[2,256,128]{2,1,0:T(8,128)(2,1)S(1)} %copy-done.73), channel_id=1, source_target_pairs={{0,8},{4,12},{8,0},{12,4},{1,9},{5,13},{9,1},{13,5},{2,10},{6,14},... | collective-permute-start | bytes 393224 | tf_op jit(solution)/shard_map/ppermute | solution.py:299
  168.5 40.6 %collective-permute-start.23 = (bf16[8,512,128]{2,1,0:T(8,128)(2,1)}, bf16[8,512,128]{2,1,0:T(8,128)(2,1)S(1)}, u32[]{:S(2)}, u32[]{:S(2)}) collective-permute-start(bf16[8,512,128]{2,1,0:T(8,128)(2,1)} %get-tuple-element.114), channel_id=1, source_target_pairs={{0,8},{4,12},{8,0},{12,4},{1,9},{5,13},{9,1},{13,5},{2,10},{6,14},... | collective-permute-start | bytes 3145736 | tf_op jit(solution)/shard_map/ppermute | solution.py:299
  171.9 7.7 %collective-permute-start.24 = (bf16[2,256,128]{2,1,0:T(8,128)(2,1)}, bf16[2,256,128]{2,1,0:T(8,128)(2,1)S(1)}, u32[]{:S(2)}, u32[]{:S(2)}) collective-permute-start(bf16[2,256,128]{2,1,0:T(8,128)(2,1)} %sums.36.refs_6_), channel_id=1, source_target_pairs={{0,2},{1,3},{2,0},{3,1},{4,6},{5,7},{6,4},{7,5},{8,10},{9,11},{10,... | collective-permute-start | bytes 393224 | tf_op jit(solution)/shard_map/ppermute | solution.py:299
  174.5 9.3 %collective-permute-start.10 = (bf16[2,512,128]{2,1,0:T(8,128)(2,1)S(1)}, bf16[2,512,128]{2,1,0:T(8,128)(2,1)S(1)}, u32[]{:S(2)}, u32[]{:S(2)}) collective-permute-start(bf16[2,512,128]{2,1,0:T(8,128)(2,1)S(1)} %copy-done.75), channel_id=1, source_target_pairs={{0,4},{4,0},{8,12},{12,8},{1,5},{5,1},{9,13},{13,9},{2,6},{6,2},{1... | collective-permute-start | bytes 786440 | tf_op jit(solution)/shard_map/ppermute | solution.py:299
  175.6 37.2 %collective-permute-start.22 = (bf16[8,512,128]{2,1,0:T(8,128)(2,1)}, bf16[8,512,128]{2,1,0:T(8,128)(2,1)S(1)}, u32[]{:S(2)}, u32[]{:S(2)}) collective-permute-start(bf16[8,512,128]{2,1,0:T(8,128)(2,1)} %get-tuple-element.108.refs_4_), channel_id=1, source_target_pairs={{0,4},{4,0},{8,12},{12,8},{1,5},{5,1},{9,13},{13,9},{2,6},{6,2},{1... | collective-permute-start | bytes 3145736 | tf_op jit(solution)/shard_map/ppermute | solution.py:299
  179.5 23.8 %collective-permute-start.9 = (bf16[2,512,128]{2,1,0:T(8,128)(2,1)S(1)}, bf16[2,512,128]{2,1,0:T(8,128)(2,1)S(1)}, u32[]{:S(2)}, u32[]{:S(2)}) collective-permute-start(bf16[2,512,128]{2,1,0:T(8,128)(2,1)S(1)} %copy-done.68), channel_id=1, source_target_pairs={{0,8},{4,12},{8,0},{12,4},{1,9},{5,13},{9,1},{13,5},{2,10},{6,14},... | collective-permute-start | bytes 786440 | tf_op jit(solution)/shard_map/ppermute | solution.py:299
  183.9 23.6 %collective-permute-start.21 = (bf16[2,512,128]{2,1,0:T(8,128)(2,1)}, bf16[2,512,128]{2,1,0:T(8,128)(2,1)S(1)}, u32[]{:S(2)}, u32[]{:S(2)}) collective-permute-start(bf16[2,512,128]{2,1,0:T(8,128)(2,1)} %get-tuple-element.111), channel_id=1, source_target_pairs={{0,4},{4,0},{8,12},{12,8},{1,5},{5,1},{9,13},{13,9},{2,6},{6,2},{1... | collective-permute-start | bytes 786440 | tf_op jit(solution)/shard_map/ppermute | solution.py:299
  203.4 33.3 %collective-permute-start.19 = (bf16[8,512,128]{2,1,0:T(8,128)(2,1)}, bf16[8,512,128]{2,1,0:T(8,128)(2,1)S(1)}, u32[]{:S(2)}, u32[]{:S(2)}) collective-permute-start(bf16[8,512,128]{2,1,0:T(8,128)(2,1)} %sums.38.refs_8_), channel_id=1, source_target_pairs={{0,1},{1,0},{2,3},{3,2},{4,5},{5,4},{6,7},{7,6},{8,9},{9,8},{10,11... | collective-permute-start | bytes 3145736 | tf_op jit(solution)/shard_map/ppermute | solution.py:299
  207.5 31.6 %collective-permute-start.29 = (bf16[8,512,128]{2,1,0:T(8,128)(2,1)}, bf16[8,512,128]{2,1,0:T(8,128)(2,1)S(1)}, u32[]{:S(2)}, u32[]{:S(2)}) collective-permute-start(bf16[8,512,128]{2,1,0:T(8,128)(2,1)} %get-tuple-element.128), channel_id=1, source_target_pairs={{0,8},{4,12},{8,0},{12,4},{1,9},{5,13},{9,1},{13,5},{2,10},{6,14},... | collective-permute-start | bytes 3145736 | tf_op jit(solution)/shard_map/ppermute | solution.py:299
  208.2 35.5 %collective-permute-start.28 = (bf16[8,512,128]{2,1,0:T(8,128)(2,1)}, bf16[8,512,128]{2,1,0:T(8,128)(2,1)S(1)}, u32[]{:S(2)}, u32[]{:S(2)}) collective-permute-start(bf16[8,512,128]{2,1,0:T(8,128)(2,1)} %get-tuple-element.110.refs_4_), channel_id=1, source_target_pairs={{0,4},{4,0},{8,12},{12,8},{1,5},{5,1},{9,13},{13,9},{2,6},{6,2},{1... | collective-permute-start | bytes 3145736 | tf_op jit(solution)/shard_map/ppermute | solution.py:299
  209.2 26.1 %collective-permute-start.20 = (bf16[2,512,128]{2,1,0:T(8,128)(2,1)S(1)}, bf16[2,512,128]{2,1,0:T(8,128)(2,1)S(1)}, u32[]{:S(2)}, u32[]{:S(2)}) collective-permute-start(bf16[2,512,128]{2,1,0:T(8,128)(2,1)S(1)} %copy-done.69), channel_id=1, source_target_pairs={{0,8},{4,12},{8,0},{12,4},{1,9},{5,13},{9,1},{13,5},{2,10},{6,14},... | collective-permute-start | bytes 786440 | tf_op jit(solution)/shard_map/ppermute | solution.py:299
  212.8 22.5 %collective-permute-start.18 = (bf16[2,512,128]{2,1,0:T(8,128)(2,1)}, bf16[2,512,128]{2,1,0:T(8,128)(2,1)S(1)}, u32[]{:S(2)}, u32[]{:S(2)}) collective-permute-start(bf16[2,512,128]{2,1,0:T(8,128)(2,1)} %sums.39.refs_6_), channel_id=1, source_target_pairs={{0,2},{1,3},{2,0},{3,1},{4,6},{5,7},{6,4},{7,5},{8,10},{9,11},{10,... | collective-permute-start | bytes 786440 | tf_op jit(solution)/shard_map/ppermute | solution.py:299
  235.3 47.8 %collective-permute-start.40 = (bf16[8,512,128]{2,1,0:T(8,128)(2,1)}, bf16[8,512,128]{2,1,0:T(8,128)(2,1)S(1)}, u32[]{:S(2)}, u32[]{:S(2)}) collective-permute-start(bf16[8,512,128]{2,1,0:T(8,128)(2,1)} %sums.41.refs_8_), channel_id=1, source_target_pairs={{0,1},{1,0},{2,3},{3,2},{4,5},{5,4},{6,7},{7,6},{8,9},{9,8},{10,11... | collective-permute-start | bytes 3145736 | tf_op jit(solution)/shard_map/ppermute | solution.py:299
  235.3 9.6 %collective-permute-start.39 = (bf16[2,512,128]{2,1,0:T(8,128)(2,1)S(1)}, bf16[2,512,128]{2,1,0:T(8,128)(2,1)S(1)}, u32[]{:S(2)}, u32[]{:S(2)}) collective-permute-start(bf16[2,512,128]{2,1,0:T(8,128)(2,1)S(1)} %copy-done.77), channel_id=1, source_target_pairs={{0,4},{4,0},{8,12},{12,8},{1,5},{5,1},{9,13},{13,9},{2,6},{6,2},{1... | collective-permute-start | bytes 786440 | tf_op jit(solution)/shard_map/ppermute | solution.py:299
  236.7 9.6 %collective-permute-start.38 = (bf16[2,512,128]{2,1,0:T(8,128)(2,1)S(1)}, bf16[2,512,128]{2,1,0:T(8,128)(2,1)S(1)}, u32[]{:S(2)}, u32[]{:S(2)}) collective-permute-start(bf16[2,512,128]{2,1,0:T(8,128)(2,1)S(1)} %copy-done.72), channel_id=1, source_target_pairs={{0,8},{4,12},{8,0},{12,4},{1,9},{5,13},{9,1},{13,5},{2,10},{6,14},... | collective-permute-start | bytes 786440 | tf_op jit(solution)/shard_map/ppermute | solution.py:299
  239.1 31.6 %collective-permute-start.35 = (bf16[2,512,128]{2,1,0:T(8,128)(2,1)}, bf16[2,512,128]{2,1,0:T(8,128)(2,1)S(1)}, u32[]{:S(2)}, u32[]{:S(2)}) collective-permute-start(bf16[2,512,128]{2,1,0:T(8,128)(2,1)} %sums.42.refs_6_), channel_id=1, source_target_pairs={{0,2},{1,3},{2,0},{3,1},{4,6},{5,7},{6,4},{7,5},{8,10},{9,11},{10,... | collective-permute-start | bytes 786440 | tf_op jit(solution)/shard_map/ppermute | solution.py:299
  243.8 30.4 %collective-permute-start.34 = (bf16[2,512,128]{2,1,0:T(8,128)(2,1)}, bf16[2,512,128]{2,1,0:T(8,128)(2,1)S(1)}, u32[]{:S(2)}, u32[]{:S(2)}) collective-permute-start(bf16[2,512,128]{2,1,0:T(8,128)(2,1)} %get-tuple-element.132), channel_id=1, source_target_pairs={{0,4},{4,0},{8,12},{12,8},{1,5},{5,1},{9,13},{13,9},{2,6},{6,2},{1... | collective-permute-start | bytes 786440 | tf_op jit(solution)/shard_map/ppermute | solution.py:299
  244.9 35.8 %collective-permute-start.37 = (bf16[8,256,128]{2,1,0:T(8,128)(2,1)}, bf16[8,256,128]{2,1,0:T(8,128)(2,1)S(1)}, u32[]{:S(2)}, u32[]{:S(2)}) collective-permute-start(bf16[8,256,128]{2,1,0:T(8,128)(2,1)} %get-tuple-element.135), channel_id=1, source_target_pairs={{0,8},{4,12},{8,0},{12,4},{1,9},{5,13},{9,1},{13,5},{2,10},{6,14},... | collective-permute-start | bytes 1572872 | tf_op jit(solution)/shard_map/ppermute | solution.py:299
  246.2 35.6 %collective-permute-start.36 = (bf16[8,256,128]{2,1,0:T(8,128)(2,1)S(1)}, bf16[8,256,128]{2,1,0:T(8,128)(2,1)S(1)}, u32[]{:S(2)}, u32[]{:S(2)}) collective-permute-start(bf16[8,256,128]{2,1,0:T(8,128)(2,1)S(1)} %copy-done.66), channel_id=1, source_target_pairs={{0,4},{4,0},{8,12},{12,8},{1,5},{5,1},{9,13},{13,9},{2,6},{6,2},{1... | collective-permute-start | bytes 1572872 | tf_op jit(solution)/shard_map/ppermute | solution.py:299
  270.7 9.3 %collective-permute-start.33 = (bf16[2,512,128]{2,1,0:T(8,128)(2,1)S(1)}, bf16[2,512,128]{2,1,0:T(8,128)(2,1)S(1)}, u32[]{:S(2)}, u32[]{:S(2)}) collective-permute-start(bf16[2,512,128]{2,1,0:T(8,128)(2,1)S(1)} %copy-done.70), channel_id=1, source_target_pairs={{0,8},{4,12},{8,0},{12,4},{1,9},{5,13},{9,1},{13,5},{2,10},{6,14},... | collective-permute-start | bytes 786440 | tf_op jit(solution)/shard_map/ppermute | solution.py:299
  274.2 29.2 %copy-start.44 = (bf16[2,512,128]{2,1,0:T(8,128)(2,1)}, bf16[2,512,128]{2,1,0:T(8,128)(2,1)S(1)}, u32[]{:S(2)}) copy-start(bf16[2,512,128]{2,1,0:T(8,128)(2,1)S(1)} %collective-permute-done.34.refs_7_.refs_8_) | copy-start | bytes 786436
  274.2 33.6 %collective-permute-start.30 = (bf16[8,512,128]{2,1,0:T(8,128)(2,1)}, bf16[8,512,128]{2,1,0:T(8,128)(2,1)S(1)}, u32[]{:S(2)}, u32[]{:S(2)}) collective-permute-start(bf16[8,512,128]{2,1,0:T(8,128)(2,1)} %sums.44.refs_6_), channel_id=1, source_target_pairs={{0,1},{1,0},{2,3},{3,2},{4,5},{5,4},{6,7},{7,6},{8,9},{9,8},{10,11... | collective-permute-start | bytes 3145736 | tf_op jit(solution)/shard_map/ppermute | solution.py:299
  280.0 23.4 %copy-start.47 = (bf16[2,512,128]{2,1,0:T(8,128)(2,1)}, bf16[2,512,128]{2,1,0:T(8,128)(2,1)S(1)}, u32[]{:S(2)}) copy-start(bf16[2,512,128]{2,1,0:T(8,128)(2,1)S(1)} %collective-permute-done.33.refs_3_) | copy-start | bytes 786436
  280.0 12.2 %collective-permute-start.27 = (bf16[8,256,128]{2,1,0:T(8,128)(2,1)}, bf16[8,256,128]{2,1,0:T(8,128)(2,1)S(1)}, u32[]{:S(2)}, u32[]{:S(2)}) collective-permute-start(bf16[8,256,128]{2,1,0:T(8,128)(2,1)} %get-tuple-element.125), channel_id=1, source_target_pairs={{0,8},{4,12},{8,0},{12,4},{1,9},{5,13},{9,1},{13,5},{2,10},{6,14},... | collective-permute-start | bytes 1572872 | tf_op jit(solution)/shard_map/ppermute | solution.py:299
  280.7 12.4 %collective-permute-start.26 = (bf16[8,256,128]{2,1,0:T(8,128)(2,1)S(1)}, bf16[8,256,128]{2,1,0:T(8,128)(2,1)S(1)}, u32[]{:S(2)}, u32[]{:S(2)}) collective-permute-start(bf16[8,256,128]{2,1,0:T(8,128)(2,1)S(1)} %copy-done.67), channel_id=1, source_target_pairs={{0,4},{4,0},{8,12},{12,8},{1,5},{5,1},{9,13},{13,9},{2,6},{6,2},{1... | collective-permute-start | bytes 1572872 | tf_op jit(solution)/shard_map/ppermute | solution.py:299
  281.8 17.1 %collective-permute-start.32 = (bf16[8,256,128]{2,1,0:T(8,128)(2,1)}, bf16[8,256,128]{2,1,0:T(8,128)(2,1)S(1)}, u32[]{:S(2)}, u32[]{:S(2)}) collective-permute-start(bf16[8,256,128]{2,1,0:T(8,128)(2,1)} %get-tuple-element.131), channel_id=1, source_target_pairs={{0,8},{4,12},{8,0},{12,4},{1,9},{5,13},{9,1},{13,5},{2,10},{6,14},... | collective-permute-start | bytes 1572872 | tf_op jit(solution)/shard_map/ppermute | solution.py:299
  283.1 17.2 %collective-permute-start.31 = (bf16[8,256,128]{2,1,0:T(8,128)(2,1)S(1)}, bf16[8,256,128]{2,1,0:T(8,128)(2,1)S(1)}, u32[]{:S(2)}, u32[]{:S(2)}) collective-permute-start(bf16[8,256,128]{2,1,0:T(8,128)(2,1)S(1)} %copy-done.54), channel_id=1, source_target_pairs={{0,4},{4,0},{8,12},{12,8},{1,5},{5,1},{9,13},{13,9},{2,6},{6,2},{1... | collective-permute-start | bytes 1572872 | tf_op jit(solution)/shard_map/ppermute | solution.py:299
  292.3 30.8 %collective-permute-start.44 = (bf16[8,256,128]{2,1,0:T(8,128)(2,1)}, bf16[8,256,128]{2,1,0:T(8,128)(2,1)S(1)}, u32[]{:S(2)}, u32[]{:S(2)}) collective-permute-start(bf16[8,256,128]{2,1,0:T(8,128)(2,1)} %sums.47.refs_10_), channel_id=1, source_target_pairs={{0,1},{1,0},{2,3},{3,2},{4,5},{5,4},{6,7},{7,6},{8,9},{9,8},{10,11... | collective-permute-start | bytes 1572872 | tf_op jit(solution)/shard_map/ppermute | solution.py:299
  293.1 23.9 %collective-permute-start.47 = (bf16[2,512,128]{2,1,0:T(8,128)(2,1)}, bf16[2,512,128]{2,1,0:T(8,128)(2,1)S(1)}, u32[]{:S(2)}, u32[]{:S(2)}) collective-permute-start(bf16[2,512,128]{2,1,0:T(8,128)(2,1)} %sums.46.refs_4_), channel_id=1, source_target_pairs={{0,2},{1,3},{2,0},{3,1},{4,6},{5,7},{6,4},{7,5},{8,10},{9,11},{10,... | collective-permute-start | bytes 786440 | tf_op jit(solution)/shard_map/ppermute | solution.py:299
  298.9 18.8 %collective-permute-start.46 = (bf16[2,512,128]{2,1,0:T(8,128)(2,1)S(1)}, bf16[2,512,128]{2,1,0:T(8,128)(2,1)S(1)}, u32[]{:S(2)}, u32[]{:S(2)}) collective-permute-start(bf16[2,512,128]{2,1,0:T(8,128)(2,1)S(1)} %copy-done.76), channel_id=1, source_target_pairs={{0,4},{4,0},{8,12},{12,8},{1,5},{5,1},{9,13},{13,9},{2,6},{6,2},{1... | collective-permute-start | bytes 786440 | tf_op jit(solution)/shard_map/ppermute | solution.py:299
  300.3 20.7 %collective-permute-start.45 = (bf16[2,512,128]{2,1,0:T(8,128)(2,1)S(1)}, bf16[2,512,128]{2,1,0:T(8,128)(2,1)S(1)}, u32[]{:S(2)}, u32[]{:S(2)}) collective-permute-start(bf16[2,512,128]{2,1,0:T(8,128)(2,1)S(1)} %copy-done.71), channel_id=1, source_target_pairs={{0,8},{4,12},{8,0},{12,4},{1,9},{5,13},{9,1},{13,5},{2,10},{6,14},... | collective-permute-start | bytes 786440 | tf_op jit(solution)/shard_map/ppermute | solution.py:299
  307.8 34.2 %collective-permute-start.42 = (bf16[8,256,128]{2,1,0:T(8,128)(2,1)}, bf16[8,256,128]{2,1,0:T(8,128)(2,1)S(1)}, u32[]{:S(2)}, u32[]{:S(2)}) collective-permute-start(bf16[8,256,128]{2,1,0:T(8,128)(2,1)} %sums.49.refs_6_), channel_id=1, source_target_pairs={{0,1},{1,0},{2,3},{3,2},{4,5},{5,4},{6,7},{7,6},{8,9},{9,8},{10,11... | collective-permute-start | bytes 1572872 | tf_op jit(solution)/shard_map/ppermute | solution.py:299
  317.0 13.7 %collective-permute-start.51 = (bf16[2,512,128]{2,1,0:T(8,128)(2,1)}, bf16[2,512,128]{2,1,0:T(8,128)(2,1)S(1)}, u32[]{:S(2)}, u32[]{:S(2)}) collective-permute-start(bf16[2,512,128]{2,1,0:T(8,128)(2,1)} %get-tuple-element.146), channel_id=1, source_target_pairs={{0,4},{4,0},{8,12},{12,8},{1,5},{5,1},{9,13},{13,9},{2,6},{6,2},{1... | collective-permute-start | bytes 786440 | tf_op jit(solution)/shard_map/ppermute | solution.py:299
  317.7 13.5 %collective-permute-start.50 = (bf16[2,512,128]{2,1,0:T(8,128)(2,1)}, bf16[2,512,128]{2,1,0:T(8,128)(2,1)S(1)}, u32[]{:S(2)}, u32[]{:S(2)}) collective-permute-start(bf16[2,512,128]{2,1,0:T(8,128)(2,1)} %get-tuple-element.140.refs_4_), channel_id=1, source_target_pairs={{0,8},{4,12},{8,0},{12,4},{1,9},{5,13},{9,1},{13,5},{2,10},{6,14},... | collective-permute-start | bytes 786440 | tf_op jit(solution)/shard_map/ppermute | solution.py:299
  321.0 32.7 %collective-permute-start.41 = (bf16[8,256,128]{2,1,0:T(8,128)(2,1)}, bf16[8,256,128]{2,1,0:T(8,128)(2,1)S(1)}, u32[]{:S(2)}, u32[]{:S(2)}) collective-permute-start(bf16[8,256,128]{2,1,0:T(8,128)(2,1)} %sums.51.refs_10_), channel_id=1, source_target_pairs={{0,1},{1,0},{2,3},{3,2},{4,5},{5,4},{6,7},{7,6},{8,9},{9,8},{10,11... | collective-permute-start | bytes 1572872 | tf_op jit(solution)/shard_map/ppermute | solution.py:299
  323.1 15.9 %collective-permute-start.43 = (bf16[2,512,128]{2,1,0:T(8,128)(2,1)S(1)}, bf16[2,512,128]{2,1,0:T(8,128)(2,1)S(1)}, u32[]{:S(2)}, u32[]{:S(2)}) collective-permute-start(bf16[2,512,128]{2,1,0:T(8,128)(2,1)S(1)} %copy-done.43), channel_id=1, source_target_pairs={{0,2},{1,3},{2,0},{3,1},{4,6},{5,7},{6,4},{7,5},{8,10},{9,11},{10,... | collective-permute-start | bytes 786440 | tf_op jit(solution)/shard_map/ppermute | solution.py:299
  330.7 5.2 %collective-permute-start.49 = (bf16[2,256,128]{2,1,0:T(8,128)(2,1)}, bf16[2,256,128]{2,1,0:T(8,128)(2,1)S(1)}, u32[]{:S(2)}, u32[]{:S(2)}) collective-permute-start(bf16[2,256,128]{2,1,0:T(8,128)(2,1)} %get-tuple-element.145), channel_id=1, source_target_pairs={{0,4},{4,0},{8,12},{12,8},{1,5},{5,1},{9,13},{13,9},{2,6},{6,2},{1... | collective-permute-start | bytes 393224 | tf_op jit(solution)/shard_map/ppermute | solution.py:299
  331.2 5.2 %collective-permute-start.48 = (bf16[2,256,128]{2,1,0:T(8,128)(2,1)}, bf16[2,256,128]{2,1,0:T(8,128)(2,1)S(1)}, u32[]{:S(2)}, u32[]{:S(2)}) collective-permute-start(bf16[2,256,128]{2,1,0:T(8,128)(2,1)} %get-tuple-element.144.refs_8_), channel_id=1, source_target_pairs={{0,8},{4,12},{8,0},{12,4},{1,9},{5,13},{9,1},{13,5},{2,10},{6,14},... | collective-permute-start | bytes 393224 | tf_op jit(solution)/shard_map/ppermute | solution.py:299
  344.7 5.2 %collective-permute-start.53 = (bf16[2,256,128]{2,1,0:T(8,128)(2,1)}, bf16[2,256,128]{2,1,0:T(8,128)(2,1)S(1)}, u32[]{:S(2)}, u32[]{:S(2)}) collective-permute-start(bf16[2,256,128]{2,1,0:T(8,128)(2,1)} %get-tuple-element.150), channel_id=1, source_target_pairs={{0,4},{4,0},{8,12},{12,8},{1,5},{5,1},{9,13},{13,9},{2,6},{6,2},{1... | collective-permute-start | bytes 393224 | tf_op jit(solution)/shard_map/ppermute | solution.py:299
  346.1 5.2 %collective-permute-start.52 = (bf16[2,256,128]{2,1,0:T(8,128)(2,1)}, bf16[2,256,128]{2,1,0:T(8,128)(2,1)S(1)}, u32[]{:S(2)}, u32[]{:S(2)}) collective-permute-start(bf16[2,256,128]{2,1,0:T(8,128)(2,1)} %get-tuple-element.149.refs_8_), channel_id=1, source_target_pairs={{0,8},{4,12},{8,0},{12,4},{1,9},{5,13},{9,1},{13,5},{2,10},{6,14},... | collective-permute-start | bytes 393224 | tf_op jit(solution)/shard_map/ppermute | solution.py:299
  347.0 20.1 %collective-permute-start.60 = (bf16[2,512,128]{2,1,0:T(8,128)(2,1)S(1)}, bf16[2,512,128]{2,1,0:T(8,128)(2,1)S(1)}, u32[]{:S(2)}, u32[]{:S(2)}) collective-permute-start(bf16[2,512,128]{2,1,0:T(8,128)(2,1)S(1)} %copy-done.40), channel_id=1, source_target_pairs={{0,2},{1,3},{2,0},{3,1},{4,6},{5,7},{6,4},{7,5},{8,10},{9,11},{10,... | collective-permute-start | bytes 786440 | tf_op jit(solution)/shard_map/ppermute | solution.py:299
  348.5 21.5 %collective-permute-start.59 = (bf16[2,512,128]{2,1,0:T(8,128)(2,1)S(1)}, bf16[2,512,128]{2,1,0:T(8,128)(2,1)S(1)}, u32[]{:S(2)}, u32[]{:S(2)}) collective-permute-start(bf16[2,512,128]{2,1,0:T(8,128)(2,1)S(1)} %copy-done.41), channel_id=1, source_target_pairs={{0,2},{1,3},{2,0},{3,1},{4,6},{5,7},{6,4},{7,5},{8,10},{9,11},{10,... | collective-permute-start | bytes 786440 | tf_op jit(solution)/shard_map/ppermute | solution.py:299
  356.5 5.2 %collective-permute-start.55 = (bf16[2,256,128]{2,1,0:T(8,128)(2,1)}, bf16[2,256,128]{2,1,0:T(8,128)(2,1)S(1)}, u32[]{:S(2)}, u32[]{:S(2)}) collective-permute-start(bf16[2,256,128]{2,1,0:T(8,128)(2,1)} %get-tuple-element.152), channel_id=1, source_target_pairs={{0,4},{4,0},{8,12},{12,8},{1,5},{5,1},{9,13},{13,9},{2,6},{6,2},{1... | collective-permute-start | bytes 393224 | tf_op jit(solution)/shard_map/ppermute | solution.py:299
  357.2 6.2 %collective-permute-start.54 = (bf16[2,256,128]{2,1,0:T(8,128)(2,1)}, bf16[2,256,128]{2,1,0:T(8,128)(2,1)S(1)}, u32[]{:S(2)}, u32[]{:S(2)}) collective-permute-start(bf16[2,256,128]{2,1,0:T(8,128)(2,1)} %get-tuple-element.151.refs_8_), channel_id=1, source_target_pairs={{0,8},{4,12},{8,0},{12,4},{1,9},{5,13},{9,1},{13,5},{2,10},{6,14},... | collective-permute-start | bytes 393224 | tf_op jit(solution)/shard_map/ppermute | solution.py:299
  358.7 14.2 %collective-permute-start.58 = (bf16[2,256,128]{2,1,0:T(8,128)(2,1)S(1)}, bf16[2,256,128]{2,1,0:T(8,128)(2,1)S(1)}, u32[]{:S(2)}, u32[]{:S(2)}) collective-permute-start(bf16[2,256,128]{2,1,0:T(8,128)(2,1)S(1)} %copy-done.58), channel_id=1, source_target_pairs={{0,2},{1,3},{2,0},{3,1},{4,6},{5,7},{6,4},{7,5},{8,10},{9,11},{10,... | collective-permute-start | bytes 393224 | tf_op jit(solution)/shard_map/ppermute | solution.py:299
  361.7 13.8 %collective-permute-start.57 = (bf16[2,256,128]{2,1,0:T(8,128)(2,1)S(1)}, bf16[2,256,128]{2,1,0:T(8,128)(2,1)S(1)}, u32[]{:S(2)}, u32[]{:S(2)}) collective-permute-start(bf16[2,256,128]{2,1,0:T(8,128)(2,1)S(1)} %copy-done.65), channel_id=1, source_target_pairs={{0,2},{1,3},{2,0},{3,1},{4,6},{5,7},{6,4},{7,5},{8,10},{9,11},{10,... | collective-permute-start | bytes 393224 | tf_op jit(solution)/shard_map/ppermute | solution.py:299
  365.8 12.3 %collective-permute-start.56 = (bf16[2,256,128]{2,1,0:T(8,128)(2,1)}, bf16[2,256,128]{2,1,0:T(8,128)(2,1)S(1)}, u32[]{:S(2)}, u32[]{:S(2)}) collective-permute-start(bf16[2,256,128]{2,1,0:T(8,128)(2,1)} %sums.59.refs_10_), channel_id=1, source_target_pairs={{0,2},{1,3},{2,0},{3,1},{4,6},{5,7},{6,4},{7,5},{8,10},{9,11},{10,... | collective-permute-start | bytes 393224 | tf_op jit(solution)/shard_map/ppermute | solution.py:299
  (76 other events, 452.8 us)
